TPU v7x, 32 devices: a whole 2x2x4 slice. The times are simulated.
32 devices in a mesh: dp: 2 (over x), row: 4 (over z), col: 4 (over y, core).
Axes of the slice: x: 2, y: 2, z: 4, core: 2. Of those that a mesh axis runs over, the one named last changes fastest.
Arguments:
- query_out: bfloat16 [384, 4096], P(('dp', 'row'), 'col'), may hold values from -6 to 6
- query_in: bfloat16 [384, 4096], P(('dp', 'col')), may hold values from -6 to 6
- out_basis: bfloat16 [4096, 4096], P('col', ('dp', 'row')), may hold values from -0.09375 to 0.09375
- in_basis: bfloat16 [4096, 4096], P(('dp', 'row'), 'col'), may hold values from -0.09375 to 0.09375
- eigvals: float32 [4096, 4096], P(('dp', 'row'), 'col'), may hold values from 16 to 1024
- train_out: bfloat16 [384, 4096], P(('dp', 'row'), 'col'), may hold values from -0.09375 to 0.09375
- train_in: bfloat16 [384, 4096], P(('dp', 'col')), may hold values from -0.09375 to 0.09375
Outputs:
- precond: float32 [4096, 4096], P(('dp', 'row'), 'col')
- scores: float32 [384], P('dp')
All inputs are finite; a program needn't handle non-finite values.
Results may differ from a plain program's by a relative error of at most 0.028.
Values may be sent and summed in bfloat16 or wider, within the bound.
A program may use at most 64 MiB of HBM per device.

v0:
```python
import functools

import jax
import jax.numpy as jnp
from jax import lax
from jax.experimental import pallas as pl
from jax.experimental.pallas import tpu as pltpu
from jax.sharding import PartitionSpec as P

damping = 1.0


def rotate_out(tok_rows, basis_panel):
    gathered = lax.all_gather(tok_rows, "row", axis=0, tiled=True)
    partial_sum = jnp.dot(gathered, basis_panel, preferred_element_type=jnp.float32)
    return lax.psum(partial_sum.astype(jnp.bfloat16), "col")


def rotate_in(tok_rows, basis_panel):
    groups = lax.axis_size("dp")
    row_count = lax.axis_size("row")
    sub_width = tok_rows.shape[1] // (groups * row_count)
    split_rows = tok_rows.reshape(tok_rows.shape[0], groups, row_count, sub_width)
    picked = lax.dynamic_index_in_dim(split_rows, lax.axis_index("row"), 2, keepdims=False)
    picked = picked.reshape(tok_rows.shape[0], groups * sub_width)
    gathered = lax.all_gather(picked, "col", axis=0, tiled=True)
    partial_sum = jnp.dot(gathered, basis_panel, preferred_element_type=jnp.float32)
    return lax.psum(partial_sum.astype(jnp.bfloat16), "row")


def wide_plan(query_out, query_in, out_basis, in_basis, eigvals, train_out, train_in):
    panel_out = lax.all_gather(out_basis, "dp", axis=1, tiled=True)
    panel_in = lax.all_gather(in_basis, "dp", axis=0, tiled=True)
    query_rot = rotate_out(query_out, panel_out)
    query_inr = rotate_in(query_in, panel_in)
    partial_grad = lax.dot_general(
        query_rot, query_inr, (((0,), (0,)), ((), ())), preferred_element_type=jnp.float32
    )
    owned = lax.psum_scatter(
        partial_grad.astype(jnp.bfloat16), "dp", scatter_dimension=0, tiled=True
    ).astype(jnp.float32)
    precond = owned / (eigvals + damping)
    shared = precond.astype(jnp.bfloat16)
    train_rot = rotate_out(train_out, panel_out)
    train_inr = rotate_in(train_in, panel_in)
    mixed = jnp.dot(
        train_rot,
        lax.all_gather(shared, "dp", axis=0, tiled=True),
        preferred_element_type=jnp.float32,
    )
    partial_scores = jnp.sum(mixed * train_inr.astype(jnp.float32), axis=1)
    scores = lax.psum(partial_scores, ("row", "col"))
    return (precond, scores)


bf16 = jnp.bfloat16
f32 = jnp.float32


def dot(left, right):
    return jnp.dot(left, right, preferred_element_type=f32)


def flat(block):
    return block.reshape(-1, block.shape[-1])


def kernel(
    q_out, q_in, basis_out_hbm, basis_in_hbm, eig_hbm, t_out, t_in,
    grad, scores,
    shared, basis_out, basis_in, eig, tin, pin, xr, zs, zr, fin, tout, pout, sr, ys, yr, rot,
    part, col_sc, row_sc, dp_sc,
    local_sem, send_sem, tin_sem, xr_sem, zr_sem, fin_sem, tout_sem, out_sem, sc_sem,
):
    d, r, c = lax.axis_index("dp"), lax.axis_index("row"), lax.axis_index("col")
    e = 1 - d
    core = lax.rem(c, 2)
    sib = c + 1 - 2 * core
    far = lax.rem(c + 2, 4)
    sibling, across, other, diagonal = (d, r, sib), (d, r, far), (e, r, c), (e, r, far)
    rows = [lax.rem(r + k, 4) for k in (1, 2, 3)]
    cols = [lax.rem(c + k, 4) for k in (1, 2, 3)]
    own_out, own_in = 4 * d + r, 4 * d + c
    toks, outs = (q_in, t_in), (q_out, t_out)
    width = basis_in.shape[0]

    loads = [
        pltpu.make_async_copy(basis_in_hbm, basis_in, local_sem.at[0]),
        pltpu.make_async_copy(basis_out_hbm, basis_out, local_sem.at[1]),
        pltpu.make_async_copy(eig_hbm, eig, local_sem.at[2]),
    ]
    for load in loads:
        load.start()

    barrier = pltpu.get_barrier_semaphore()
    peers = [(d, r, j) for j in cols] + [(d, j, c) for j in rows] + [other, diagonal]
    for peer in peers:
        pl.semaphore_signal(barrier, inc=1, device_id=peer, device_id_type=pl.DeviceIdType.MESH)
    pl.semaphore_wait(barrier, len(peers))

    sends = []

    def send(src, dst, sem, peer):
        copy = pltpu.make_async_remote_copy(
            src_ref=src, dst_ref=dst, send_sem=send_sem.at[len(sends)], recv_sem=sem,
            device_id=peer, device_id_type=pl.DeviceIdType.MESH,
        )
        copy.start()
        sends.append(copy)

    def got(dst, sem):
        pltpu.make_async_remote_copy(
            src_ref=dst, dst_ref=dst, send_sem=send_sem.at[0], recv_sem=sem,
            device_id=sibling, device_id_type=pl.DeviceIdType.MESH,
        ).wait_recv()

    def columns(ref, group):
        return ref.at[:, pl.ds(pl.multiple_of((group * 4 + r) * width, width), width)]

    mine, held = [], {}
    for ch in range(2):
        for peer in (other, across, diagonal, sibling):
            send(columns(toks[ch], peer[0]), tin.at[ch, own_in], tin_sem.at[ch, own_in], peer)
        keep = pltpu.make_async_copy(columns(toks[ch], d), tin.at[ch, own_in], local_sem.at[3 + ch])
        keep.start()
        mine.append(keep)

    def spread_out(ch):
        for j in rows:
            send(outs[ch], tout.at[ch, own_out], tout_sem.at[ch, own_out], (d, j, c))

        keep = pltpu.make_async_copy(outs[ch], tout.at[ch, own_out], local_sem.at[5 + ch])
        keep.start()
        held[ch] = keep

    def share_tokens(ch):
        for slot in (4 * e + c, 4 * d + far, 4 * e + far):
            got(tin.at[ch, slot], tin_sem.at[ch, slot])
            send(tin.at[ch, slot], tin.at[ch, slot], tin_sem.at[ch, slot], sibling)

    def rotate_in_part(ch):
        sib_far = lax.rem(sib + 2, 4)
        for slot in (4 * d + sib, 4 * e + sib, 4 * d + sib_far, 4 * e + sib_far):
            got(tin.at[ch, slot], tin_sem.at[ch, slot])
        mine[ch].wait()
        if ch == 0:
            loads[0].wait()
        for half in (e, d):
            block = flat(tin[ch, pl.ds(4 * half, 4)])
            value = dot(block, basis_in[...]).astype(bf16)
            pin[ch, pl.ds(4 * half, 4)] = value.reshape(4, -1, value.shape[-1])
            if half is e:
                for j in rows + [r]:
                    send(pin.at[ch, 4 * e + j], xr.at[ch, j], xr_sem.at[ch, j], other)

    def scatter_rows(ch):
        for j in rows + [r]:
            got(xr.at[ch, j], xr_sem.at[ch, j])
            zs[ch, j] = (pin[ch, 4 * d + j].astype(f32) + xr[ch, j].astype(f32)).astype(bf16)
            if j is not r:
                send(zs.at[ch, j], zr.at[ch, r], zr_sem.at[ch, r], (d, j, c))

    def finish_piece(ch):
        total = zs[ch, r].astype(f32)
        for j in rows:
            got(zr.at[ch, j], zr_sem.at[ch, j])
            total = total + zr[ch, j].astype(f32)
        fin[ch, own_out] = total.astype(bf16)
        for peer in [(d, j, c) for j in rows] + [other]:
            send(fin.at[ch, own_out], fin.at[ch, own_out], fin_sem.at[ch, own_out], peer)

    def forward(buf, sem, ch):
        for j in rows:
            slot = 4 * d + j
            got(buf.at[ch, slot], sem.at[ch, slot])
            send(buf.at[ch, slot], buf.at[ch, slot], sem.at[ch, slot], other)

    def arrive(buf, sem, ch):
        for j in range(4):
            got(buf.at[ch, 4 * e + j], sem.at[ch, 4 * e + j])

    near, away = pl.ds(4 * core, 4), pl.ds(4 * (1 - core), 4)

    def rotate_out_part(ch):
        arrive(tout, tout_sem, ch)
        held[ch].wait()
        if ch == 0:
            loads[1].wait()
        for part_rows in (away, near):
            value = dot(flat(tout[ch, part_rows]), basis_out[...]).astype(bf16)
            pout[ch, part_rows] = value.reshape(4, -1, value.shape[-1])
            if part_rows is away:
                send(pout.at[ch, away], sr.at[ch], out_sem.at[ch, 0], sibling)

    def add_sibling(ch):
        got(sr.at[ch], out_sem.at[ch, 0])
        ys[ch] = (pout[ch, near].astype(f32) + sr[ch].astype(f32)).astype(bf16)
        send(ys.at[ch], yr.at[ch], out_sem.at[ch, 1], across)

    def add_across(ch):
        got(yr.at[ch], out_sem.at[ch, 1])
        rot[ch, near] = (ys[ch].astype(f32) + yr[ch].astype(f32)).astype(bf16)
        send(rot.at[ch, near], rot.at[ch, near], out_sem.at[ch, 2], sibling)

    def forward_out(ch):
        send(outs[ch], tout.at[ch, own_out], tout_sem.at[ch, own_out], other)
        forward(tout, tout_sem, ch)

    spread_out(0)
    share_tokens(0)
    rotate_in_part(0)
    share_tokens(1)
    rotate_in_part(1)
    scatter_rows(0)
    forward_out(0)
    scatter_rows(1)
    spread_out(1)
    finish_piece(0)
    rotate_out_part(0)
    finish_piece(1)
    add_sibling(0)
    forward(fin, fin_sem, 0)
    add_across(0)
    forward_out(1)
    forward(fin, fin_sem, 1)
    rotate_out_part(1)
    add_sibling(1)

    arrive(fin, fin_sem, 0)
    got(rot.at[0, away], out_sem.at[0, 2])
    loads[2].wait()
    value = lax.dot_general(
        flat(rot[0]), flat(fin[0]), (((0,), (0,)), ((), ())), preferred_element_type=f32
    )
    grad[...] = value.astype(bf16)
    shared[...] = (value / (eig[...] + damping)).astype(bf16)

    add_across(1)
    got(rot.at[1, away], out_sem.at[1, 2])
    mixed = dot(flat(rot[1]), shared[...])
    arrive(fin, fin_sem, 1)
    product = mixed * flat(fin[1]).astype(f32)
    lanes = product[:, :128]
    for at in range(128, product.shape[1], 128):
        lanes = lanes + product[:, at:at + 128]
    line = jnp.sum(lanes.T, axis=0, keepdims=True)
    kept = line.shape[1] // 2
    part[0] = jnp.broadcast_to(line[:, :kept], part.shape[1:])
    part[1] = jnp.broadcast_to(line[:, kept:], part.shape[1:])

    col_sc[c] = part[...]
    for j in cols:
        send(part, col_sc.at[c], sc_sem.at[c], (d, r, j))
    for j in cols:
        got(col_sc.at[j], sc_sem.at[j])
    row_sc[r] = ((col_sc[0] + col_sc[1]) + col_sc[2]) + col_sc[3]
    for j in rows:
        send(row_sc.at[r], row_sc.at[r], sc_sem.at[4 + r], (d, j, c))
    for j in rows:
        got(row_sc.at[j], sc_sem.at[4 + j])
    dp_sc[0:2] = ((row_sc[0] + row_sc[1]) + row_sc[2]) + row_sc[3]
    send(dp_sc.at[e], dp_sc.at[2], sc_sem.at[8], other)
    got(dp_sc.at[2], sc_sem.at[8])
    scores[...] = dp_sc[d, 0:1] + dp_sc[2, 0:1]

    for copy in sends:
        copy.wait_send()


def local_plan(query_out, query_in, out_basis, in_basis, eigvals, train_out, train_in):
    own, wide = query_out.shape
    depth, across = in_basis.shape
    narrow = out_basis.shape[1]
    slots = lax.axis_size("dp") * lax.axis_size("row")
    kept = own * lax.axis_size("row")
    vmem = pl.BlockSpec(memory_space=pltpu.VMEM)
    hbm = pl.BlockSpec(memory_space=pl.ANY)
    dma = pltpu.SemaphoreType.DMA
    grad, scores = pl.pallas_call(
        kernel,
        out_shape=(
            jax.ShapeDtypeStruct(eigvals.shape, bf16),
            jax.ShapeDtypeStruct((1, kept), f32),
        ),
        in_specs=[hbm] * 7,
        out_specs=(vmem, vmem),
        scratch_shapes=[
            pltpu.VMEM(eigvals.shape, bf16),
            pltpu.VMEM(out_basis.shape, bf16),
            pltpu.VMEM(in_basis.shape, bf16),
            pltpu.VMEM(eigvals.shape, f32),
            pltpu.VMEM((2, slots, own, depth), bf16),
            pltpu.VMEM((2, slots, own, across), bf16),
            pltpu.VMEM((2, 4, own, across), bf16),
            pltpu.VMEM((2, 4, own, across), bf16),
            pltpu.VMEM((2, 4, own, across), bf16),
            pltpu.VMEM((2, slots, own, across), bf16),
            pltpu.VMEM((2, slots, own, wide), bf16),
            pltpu.VMEM((2, slots, own, narrow), bf16),
            pltpu.VMEM((2, 4, own, narrow), bf16),
            pltpu.VMEM((2, 4, own, narrow), bf16),
            pltpu.VMEM((2, 4, own, narrow), bf16),
            pltpu.VMEM((2, slots, own, narrow), bf16),
            pltpu.VMEM((2, 8, kept), f32),
            pltpu.VMEM((4, 2, 8, kept), f32),
            pltpu.VMEM((4, 2, 8, kept), f32),
            pltpu.VMEM((3, 8, kept), f32),
            dma((7,)),
            dma((80,)),
            dma((2, 8)),
            dma((2, 4)),
            dma((2, 4)),
            dma((2, 8)),
            dma((2, 8)),
            dma((2, 3)),
            dma((9,)),
        ],
        compiler_params=pltpu.CompilerParams(
            collective_id=0, has_side_effects=True, vmem_limit_bytes=63 * 2**20
        ),
        cost_estimate=pl.CostEstimate(flops=4 * 10**9, bytes_accessed=10**7, transcendentals=0),
    )(query_out, query_in, out_basis, in_basis, eigvals, train_out, train_in)
    return (grad.astype(f32) / (eigvals + damping), scores.reshape(kept))


def fits(mesh):
    return dict(mesh.shape) == {"dp": 2, "row": 4, "col": 4}


def solution(mesh):
    in_specs = (
        P(("dp", "row"), "col"),
        P(("dp", "col"), None),
        P("col", ("dp", "row")),
        P(("dp", "row"), "col"),
        P(("dp", "row"), "col"),
        P(("dp", "row"), "col"),
        P(("dp", "col"), None),
    )
    out_specs = (P(("dp", "row"), "col"), P("dp"))
    return jax.shard_map(
        local_plan if fits(mesh) else wide_plan, mesh=mesh, in_specs=in_specs, out_specs=out_specs, check_vma=False
    )
```

profile of v0, /device:TPU:0, one launch (start us, length us, event | category | flops | bytes accessed | tf_op | source)
XLA Modules:
  0.0 98.2 jit_solution(17531754071402963819)
XLA Ops:
  0.6 93.4 %shard_map.86 = (bf16[512,1024]{1,0:T(8,128)(2,1)}, f32[1,192]{1,0:T(1,128)}) custom-call(bf16[48,1024]{1,0:T(8,128)(2,1)} %q_out.1, bf16[48,4096]{1,0:T(8,128)(2,1)} %q_in.1, bf16[1024,512]{1,0:T(8,128)(2,1)} %basis_out_hbm.1, bf16[512,1024]{1,0:T(8,128)(2,1)} %basis_in_hbm.1, f32[512,1024]{1,0:T(8,128)} %eig_hbm.1, bf16[48,1024]{1,0:T(8,128)(2,1)} %t_out.1, ...), custom_call_target="tpu_custom_call" | custom-call | flops 4000000000 | bytes 10000000 | tf_op jit(solution)/shard_map/pallas_call | solution.py:279
  94.0 0.0 copy-start
  94.0 3.6 %add_divide_fusion = f32[512,1024]{1,0:T(8,128)} fusion(f32[512,1024]{1,0:T(8,128)} %eig_hbm.1, bf16[512,1024]{1,0:T(8,128)(2,1)} %get-tuple-element.4), kind=kLoop, calls=%fused_computation | loop fusion | flops 1572864 | bytes 5242880 | tf_op jit(solution)/shard_map/div | solution.py:323
  97.7 0.0 copy-done
  97.7 0.6 copy.10
Async XLA Ops:
  94.0 3.6 %copy-start = (f32[1,192]{1,0:T(1,128)S(1)}, f32[1,192]{1,0:T(1,128)}, u32[]{:S(2)}) copy-start(f32[1,192]{1,0:T(1,128)} %get-tuple-element.5) | copy-start | bytes 2308
where the time goes:
time: 98.4 us; the launch traced here: 98.2 us
  Pallas kernels  93.4 us (95%)
  other arithmetic  3.63 us (4%)
    pallas_call x1, Pallas kernels, local_plan(): pl.pallas_call(kernel, out_shape=(jax.ShapeDtypeStruct(eigvals.shape, bf1...  93.4 us
    div x1, other arithmetic, local_plan(): return (grad.astype(f32) / (eigvals + damping), scores.reshape(kept))  3.63 us

commit v1 on v0

--- a/solution.py
+++ b/solution.py
@@ -66,9 +66,9 @@
 
 
 def kernel(
-    q_out, q_in, basis_out_hbm, basis_in_hbm, eig_hbm, t_out, t_in,
+    q_out_hbm, q_in_hbm, basis_out_hbm, basis_in_hbm, eig_hbm, t_out_hbm, t_in_hbm,
     grad, scores,
-    shared, basis_out, basis_in, eig, tin, pin, xr, zs, zr, fin, tout, pout, sr, ys, yr, rot,
+    q_in, t_in, q_out, t_out, shared, basis_out, basis_in, eig, tin, pin, xr, zs, zr, fin, tout, pout, sr, ys, yr, rot,
     part, col_sc, row_sc, dp_sc,
     local_sem, send_sem, tin_sem, xr_sem, zr_sem, fin_sem, tout_sem, out_sem, sc_sem,
 ):
@@ -89,7 +89,13 @@
         pltpu.make_async_copy(basis_out_hbm, basis_out, local_sem.at[1]),
         pltpu.make_async_copy(eig_hbm, eig, local_sem.at[2]),
     ]
-    for load in loads:
+    tokens = [
+        pltpu.make_async_copy(src, dst, local_sem.at[7 + k])
+        for k, (src, dst) in enumerate(
+            ((q_in_hbm, q_in), (t_in_hbm, t_in), (q_out_hbm, q_out), (t_out_hbm, t_out))
+        )
+    ]
+    for load in tokens + loads:
         load.start()
 
     barrier = pltpu.get_barrier_semaphore()
@@ -119,6 +125,7 @@
 
     mine, held = [], {}
     for ch in range(2):
+        tokens[ch].wait()
         for peer in (other, across, diagonal, sibling):
             send(columns(toks[ch], peer[0]), tin.at[ch, own_in], tin_sem.at[ch, own_in], peer)
         keep = pltpu.make_async_copy(columns(toks[ch], d), tin.at[ch, own_in], local_sem.at[3 + ch])
@@ -126,6 +133,7 @@
         mine.append(keep)
 
     def spread_out(ch):
+        tokens[2 + ch].wait()
         for j in rows:
             send(outs[ch], tout.at[ch, own_out], tout_sem.at[ch, own_out], (d, j, c))
 
@@ -207,6 +215,7 @@
         forward(tout, tout_sem, ch)
 
     spread_out(0)
+    spread_out(1)
     share_tokens(0)
     rotate_in_part(0)
     share_tokens(1)
@@ -214,17 +223,16 @@
     scatter_rows(0)
     forward_out(0)
     scatter_rows(1)
-    spread_out(1)
     finish_piece(0)
+    forward_out(1)
     rotate_out_part(0)
+    add_sibling(0)
     finish_piece(1)
-    add_sibling(0)
     forward(fin, fin_sem, 0)
     add_across(0)
-    forward_out(1)
-    forward(fin, fin_sem, 1)
     rotate_out_part(1)
     add_sibling(1)
+    forward(fin, fin_sem, 1)
 
     arrive(fin, fin_sem, 0)
     got(rot.at[0, away], out_sem.at[0, 2])
@@ -285,6 +293,10 @@
         in_specs=[hbm] * 7,
         out_specs=(vmem, vmem),
         scratch_shapes=[
+            pltpu.VMEM(query_in.shape, bf16),
+            pltpu.VMEM(query_in.shape, bf16),
+            pltpu.VMEM(query_out.shape, bf16),
+            pltpu.VMEM(query_out.shape, bf16),
             pltpu.VMEM(eigvals.shape, bf16),
             pltpu.VMEM(out_basis.shape, bf16),
             pltpu.VMEM(in_basis.shape, bf16),
@@ -305,7 +317,7 @@
             pltpu.VMEM((4, 2, 8, kept), f32),
             pltpu.VMEM((4, 2, 8, kept), f32),
             pltpu.VMEM((3, 8, kept), f32),
-            dma((7,)),
+            dma((11,)),
             dma((80,)),
             dma((2, 8)),
             dma((2, 4)),

time: 98.4 us -> 82.6 us (0.84)
  Pallas kernels: 93.4 us -> 77.6 us
    pallas_call x1, Pallas kernels: 93.4 us -> 77.6 us  [local_plan(): pl.pallas_call(kernel, out_shape=(jax.ShapeDtypeStruct(eigvals.shape, bf1...]
where the time goes in v1:
time: 82.6 us; the launch traced here: 82.5 us
  Pallas kernels  77.6 us (94%)
  other arithmetic  3.63 us (4%)
    pallas_call x1, Pallas kernels, local_plan(): pl.pallas_call(kernel, out_shape=(jax.ShapeDtypeStruct(eigvals.shape, bf1...  77.6 us
    div x1, other arithmetic, local_plan(): return (grad.astype(f32) / (eigvals + damping), scores.reshape(kept))  3.63 us

profile of v1, /device:TPU:0, one launch (start us, length us, event | category | flops | bytes accessed | tf_op | source)
XLA Modules:
  0.0 82.5 jit_solution(4950894407382083409)
XLA Ops:
  0.6 77.6 %shard_map.86 = (bf16[512,1024]{1,0:T(8,128)(2,1)}, f32[1,192]{1,0:T(1,128)}) custom-call(bf16[48,1024]{1,0:T(8,128)(2,1)} %q_out_hbm.1, bf16[48,4096]{1,0:T(8,128)(2,1)} %q_in_hbm.1, bf16[1024,512]{1,0:T(8,128)(2,1)} %basis_out_hbm.1, bf16[512,1024]{1,0:T(8,128)(2,1)} %basis_in_hbm.1, f32[512,1024]{1,0:T(8,128)} %eig_hbm.1, bf16[48,1024]{1,0:T(8,128)(2,1)} %t_out_hbm.1, ...), custom_call_target="tpu_custom_call" | custom-call | flops 4000000000 | bytes 10000000 | tf_op jit(solution)/shard_map/pallas_call | solution.py:287
  78.3 0.0 copy-start
  78.3 3.6 %add_divide_fusion = f32[512,1024]{1,0:T(8,128)} fusion(f32[512,1024]{1,0:T(8,128)} %eig_hbm.1, bf16[512,1024]{1,0:T(8,128)(2,1)} %get-tuple-element.4), kind=kLoop, calls=%fused_computation | loop fusion | flops 1572864 | bytes 5242880 | tf_op jit(solution)/shard_map/div | solution.py:335
  81.9 0.0 copy-done
  81.9 0.6 copy.10
Async XLA Ops:
  78.3 3.6 %copy-start = (f32[1,192]{1,0:T(1,128)S(1)}, f32[1,192]{1,0:T(1,128)}, u32[]{:S(2)}) copy-start(f32[1,192]{1,0:T(1,128)} %get-tuple-element.5) | copy-start | bytes 2308

commit v2 on v1

--- a/solution.py
+++ b/solution.py
@@ -77,10 +77,10 @@
     core = lax.rem(c, 2)
     sib = c + 1 - 2 * core
     far = lax.rem(c + 2, 4)
-    sibling, across, other, diagonal = (d, r, sib), (d, r, far), (e, r, c), (e, r, far)
+    sibling, across, other = (d, r, sib), (d, r, far), (e, r, c)
     rows = [lax.rem(r + k, 4) for k in (1, 2, 3)]
     cols = [lax.rem(c + k, 4) for k in (1, 2, 3)]
-    own_out, own_in = 4 * d + r, 4 * d + c
+    own_out, own_in, kept_row = 4 * d + r, 4 * d + c, 4 * e + r
     toks, outs = (q_in, t_in), (q_out, t_out)
     width = basis_in.shape[0]
 
@@ -99,7 +99,7 @@
         load.start()
 
     barrier = pltpu.get_barrier_semaphore()
-    peers = [(d, r, j) for j in cols] + [(d, j, c) for j in rows] + [other, diagonal]
+    peers = [(d, r, j) for j in cols] + [(d, j, c) for j in rows] + [other]
     for peer in peers:
         pl.semaphore_signal(barrier, inc=1, device_id=peer, device_id_type=pl.DeviceIdType.MESH)
     pl.semaphore_wait(barrier, len(peers))
@@ -126,7 +126,7 @@
     mine, held = [], {}
     for ch in range(2):
         tokens[ch].wait()
-        for peer in (other, across, diagonal, sibling):
+        for peer in (other, across, sibling):
             send(columns(toks[ch], peer[0]), tin.at[ch, own_in], tin_sem.at[ch, own_in], peer)
         keep = pltpu.make_async_copy(columns(toks[ch], d), tin.at[ch, own_in], local_sem.at[3 + ch])
         keep.start()
@@ -141,30 +141,31 @@
         keep.start()
         held[ch] = keep
 
-    def share_tokens(ch):
-        for slot in (4 * e + c, 4 * d + far, 4 * e + far):
+    sib_far = lax.rem(sib + 2, 4)
+
+    def pass_tokens(ch, slot, targets):
+        got(tin.at[ch, slot], tin_sem.at[ch, slot])
+        for peer in targets:
+            send(tin.at[ch, slot], tin.at[ch, slot], tin_sem.at[ch, slot], peer)
+
+    def rotate_half(ch, half):
+        for slot in (4 * half + sib, 4 * half + sib_far):
             got(tin.at[ch, slot], tin_sem.at[ch, slot])
-            send(tin.at[ch, slot], tin.at[ch, slot], tin_sem.at[ch, slot], sibling)
-
-    def rotate_in_part(ch):
-        sib_far = lax.rem(sib + 2, 4)
-        for slot in (4 * d + sib, 4 * e + sib, 4 * d + sib_far, 4 * e + sib_far):
-            got(tin.at[ch, slot], tin_sem.at[ch, slot])
+        value = dot(flat(tin[ch, pl.ds(4 * half, 4)]), basis_in[...]).astype(bf16)
+        pin[ch, pl.ds(4 * half, 4)] = value.reshape(4, -1, value.shape[-1])
+
+    def rotate_own(ch):
         mine[ch].wait()
         if ch == 0:
             loads[0].wait()
-        for half in (e, d):
-            block = flat(tin[ch, pl.ds(4 * half, 4)])
-            value = dot(block, basis_in[...]).astype(bf16)
-            pin[ch, pl.ds(4 * half, 4)] = value.reshape(4, -1, value.shape[-1])
-            if half is e:
-                for j in rows + [r]:
-                    send(pin.at[ch, 4 * e + j], xr.at[ch, j], xr_sem.at[ch, j], other)
+        rotate_half(ch, d)
+        for j in rows + [r]:
+            send(pin.at[ch, 4 * d + j], xr.at[ch, j], xr_sem.at[ch, j], other)
 
     def scatter_rows(ch):
         for j in rows + [r]:
             got(xr.at[ch, j], xr_sem.at[ch, j])
-            zs[ch, j] = (pin[ch, 4 * d + j].astype(f32) + xr[ch, j].astype(f32)).astype(bf16)
+            zs[ch, j] = (pin[ch, 4 * e + j].astype(f32) + xr[ch, j].astype(f32)).astype(bf16)
             if j is not r:
                 send(zs.at[ch, j], zr.at[ch, r], zr_sem.at[ch, r], (d, j, c))
 
@@ -173,24 +174,24 @@
         for j in rows:
             got(zr.at[ch, j], zr_sem.at[ch, j])
             total = total + zr[ch, j].astype(f32)
-        fin[ch, own_out] = total.astype(bf16)
+        fin[ch, kept_row] = total.astype(bf16)
         for peer in [(d, j, c) for j in rows] + [other]:
-            send(fin.at[ch, own_out], fin.at[ch, own_out], fin_sem.at[ch, own_out], peer)
-
-    def forward(buf, sem, ch):
+            send(fin.at[ch, kept_row], fin.at[ch, kept_row], fin_sem.at[ch, kept_row], peer)
+
+    def forward(buf, sem, ch, half):
         for j in rows:
-            slot = 4 * d + j
+            slot = 4 * half + j
             got(buf.at[ch, slot], sem.at[ch, slot])
             send(buf.at[ch, slot], buf.at[ch, slot], sem.at[ch, slot], other)
 
-    def arrive(buf, sem, ch):
+    def arrive(buf, sem, ch, half):
         for j in range(4):
-            got(buf.at[ch, 4 * e + j], sem.at[ch, 4 * e + j])
+            got(buf.at[ch, 4 * half + j], sem.at[ch, 4 * half + j])
 
     near, away = pl.ds(4 * core, 4), pl.ds(4 * (1 - core), 4)
 
     def rotate_out_part(ch):
-        arrive(tout, tout_sem, ch)
+        arrive(tout, tout_sem, ch, e)
         held[ch].wait()
         if ch == 0:
             loads[1].wait()
@@ -210,31 +211,38 @@
         rot[ch, near] = (ys[ch].astype(f32) + yr[ch].astype(f32)).astype(bf16)
         send(rot.at[ch, near], rot.at[ch, near], out_sem.at[ch, 2], sibling)
 
-    def forward_out(ch):
+    def send_own_out(ch):
         send(outs[ch], tout.at[ch, own_out], tout_sem.at[ch, own_out], other)
-        forward(tout, tout_sem, ch)
 
     spread_out(0)
+    send_own_out(0)
     spread_out(1)
-    share_tokens(0)
-    rotate_in_part(0)
-    share_tokens(1)
-    rotate_in_part(1)
+    pass_tokens(0, 4 * d + far, [sibling])
+    rotate_own(0)
+    pass_tokens(1, 4 * d + far, [sibling])
+    rotate_own(1)
+    for ch in range(2):
+        pass_tokens(ch, 4 * e + c, [across, sibling])
+    for ch in range(2):
+        pass_tokens(ch, 4 * e + far, [sibling])
+    for ch in range(2):
+        rotate_half(ch, e)
     scatter_rows(0)
-    forward_out(0)
+    forward(tout, tout_sem, 0, d)
     scatter_rows(1)
     finish_piece(0)
-    forward_out(1)
+    send_own_out(1)
+    forward(tout, tout_sem, 1, d)
     rotate_out_part(0)
     add_sibling(0)
     finish_piece(1)
-    forward(fin, fin_sem, 0)
+    forward(fin, fin_sem, 0, e)
     add_across(0)
     rotate_out_part(1)
     add_sibling(1)
-    forward(fin, fin_sem, 1)
-
-    arrive(fin, fin_sem, 0)
+    forward(fin, fin_sem, 1, e)
+
+    arrive(fin, fin_sem, 0, d)
     got(rot.at[0, away], out_sem.at[0, 2])
     loads[2].wait()
     value = lax.dot_general(
@@ -246,7 +254,7 @@
     add_across(1)
     got(rot.at[1, away], out_sem.at[1, 2])
     mixed = dot(flat(rot[1]), shared[...])
-    arrive(fin, fin_sem, 1)
+    arrive(fin, fin_sem, 1, d)
     product = mixed * flat(fin[1]).astype(f32)
     lanes = product[:, :128]
     for at in range(128, product.shape[1], 128):

time: 82.6 us -> 82.5 us (level)
  no operation moved by 1% of the time
where the time goes in v2:
time: 82.5 us; the launch traced here: 82.4 us
  Pallas kernels  77.5 us (94%)
  other arithmetic  3.63 us (4%)
    pallas_call x1, Pallas kernels, local_plan(): pl.pallas_call(kernel, out_shape=(jax.ShapeDtypeStruct(eigvals.shape, bf1...  77.5 us
    div x1, other arithmetic, local_plan(): return (grad.astype(f32) / (eigvals + damping), scores.reshape(kept))  3.63 us

profile of v2, /device:TPU:0, one launch (start us, length us, event | category | flops | bytes accessed | tf_op | source)
XLA Modules:
  0.0 82.4 jit_solution(7486834382477734524)
XLA Ops:
  0.6 77.5 %shard_map.86 = (bf16[512,1024]{1,0:T(8,128)(2,1)}, f32[1,192]{1,0:T(1,128)}) custom-call(bf16[48,1024]{1,0:T(8,128)(2,1)} %q_out_hbm.1, bf16[48,4096]{1,0:T(8,128)(2,1)} %q_in_hbm.1, bf16[1024,512]{1,0:T(8,128)(2,1)} %basis_out_hbm.1, bf16[512,1024]{1,0:T(8,128)(2,1)} %basis_in_hbm.1, f32[512,1024]{1,0:T(8,128)} %eig_hbm.1, bf16[48,1024]{1,0:T(8,128)(2,1)} %t_out_hbm.1, ...), custom_call_target="tpu_custom_call" | custom-call | flops 4000000000 | bytes 10000000 | tf_op jit(solution)/shard_map/pallas_call | solution.py:295
  78.2 0.0 copy-start
  78.2 3.6 %add_divide_fusion = f32[512,1024]{1,0:T(8,128)} fusion(f32[512,1024]{1,0:T(8,128)} %eig_hbm.1, bf16[512,1024]{1,0:T(8,128)(2,1)} %get-tuple-element.4), kind=kLoop, calls=%fused_computation | loop fusion | flops 1572864 | bytes 5242880 | tf_op jit(solution)/shard_map/div | solution.py:343
  81.8 0.0 copy-done
  81.8 0.6 copy.10
Async XLA Ops:
  78.2 3.6 %copy-start = (f32[1,192]{1,0:T(1,128)S(1)}, f32[1,192]{1,0:T(1,128)}, u32[]{:S(2)}) copy-start(f32[1,192]{1,0:T(1,128)} %get-tuple-element.5) | copy-start | bytes 2308

commit v3 on v2

--- a/solution.py
+++ b/solution.py
@@ -79,6 +79,8 @@
     far = lax.rem(c + 2, 4)
     sibling, across, other = (d, r, sib), (d, r, far), (e, r, c)
     rows = [lax.rem(r + k, 4) for k in (1, 2, 3)]
+    ring = [lax.rem(r + k, 4) for k in (3, 2, 1, 0)]
+    onward = (d, lax.rem(r + 1, 4), c)
     cols = [lax.rem(c + k, 4) for k in (1, 2, 3)]
     own_out, own_in, kept_row = 4 * d + r, 4 * d + c, 4 * e + r
     toks, outs = (q_in, t_in), (q_out, t_out)
@@ -159,24 +161,29 @@
         if ch == 0:
             loads[0].wait()
         rotate_half(ch, d)
-        for j in rows + [r]:
+        for j in ring:
             send(pin.at[ch, 4 * d + j], xr.at[ch, j], xr_sem.at[ch, j], other)
 
-    def scatter_rows(ch):
-        for j in rows + [r]:
-            got(xr.at[ch, j], xr_sem.at[ch, j])
-            zs[ch, j] = (pin[ch, 4 * e + j].astype(f32) + xr[ch, j].astype(f32)).astype(bf16)
-            if j is not r:
-                send(zs.at[ch, j], zr.at[ch, r], zr_sem.at[ch, r], (d, j, c))
-
-    def finish_piece(ch):
-        total = zs[ch, r].astype(f32)
-        for j in rows:
+    def scatter_step(ch, k):
+        j = ring[k]
+        got(xr.at[ch, j], xr_sem.at[ch, j])
+        total = pin[ch, 4 * e + j].astype(f32) + xr[ch, j].astype(f32)
+        if k > 0:
             got(zr.at[ch, j], zr_sem.at[ch, j])
             total = total + zr[ch, j].astype(f32)
-        fin[ch, kept_row] = total.astype(bf16)
-        for peer in [(d, j, c) for j in rows] + [other]:
-            send(fin.at[ch, kept_row], fin.at[ch, kept_row], fin_sem.at[ch, kept_row], peer)
+        if k < 3:
+            zs[ch, j] = total.astype(bf16)
+            send(zs.at[ch, j], zr.at[ch, j], zr_sem.at[ch, j], onward)
+        else:
+            fin[ch, kept_row] = total.astype(bf16)
+            for peer in (onward, other):
+                send(fin.at[ch, kept_row], fin.at[ch, kept_row], fin_sem.at[ch, kept_row], peer)
+
+    def gather_step(ch, k):
+        slot = 4 * e + ring[k]
+        got(fin.at[ch, slot], fin_sem.at[ch, slot])
+        for peer in (onward, other) if k < 2 else (other,):
+            send(fin.at[ch, slot], fin.at[ch, slot], fin_sem.at[ch, slot], peer)
 
     def forward(buf, sem, ch, half):
         for j in rows:
@@ -227,20 +234,23 @@
         pass_tokens(ch, 4 * e + far, [sibling])
     for ch in range(2):
         rotate_half(ch, e)
-    scatter_rows(0)
+    for k in range(4):
+        scatter_step(0, k)
     forward(tout, tout_sem, 0, d)
-    scatter_rows(1)
-    finish_piece(0)
+    for k in range(3):
+        scatter_step(1, k)
+        gather_step(0, k)
+    scatter_step(1, 3)
     send_own_out(1)
     forward(tout, tout_sem, 1, d)
     rotate_out_part(0)
     add_sibling(0)
-    finish_piece(1)
-    forward(fin, fin_sem, 0, e)
+    gather_step(1, 0)
     add_across(0)
+    gather_step(1, 1)
     rotate_out_part(1)
     add_sibling(1)
-    forward(fin, fin_sem, 1, e)
+    gather_step(1, 2)
 
     arrive(fin, fin_sem, 0, d)
     got(rot.at[0, away], out_sem.at[0, 2])

time: 82.5 us -> 85.3 us (1.034)
  Pallas kernels: 77.5 us -> 80.3 us
    pallas_call x1, Pallas kernels: 77.5 us -> 80.3 us  [local_plan(): pl.pallas_call(kernel, out_shape=(jax.ShapeDtypeStruct(eigvals.shape, bf1...]
where the time goes in v3:
time: 85.3 us; the launch traced here: 85.2 us
  Pallas kernels  80.3 us (94%)
  other arithmetic  3.63 us (4%)
    pallas_call x1, Pallas kernels, local_plan(): pl.pallas_call(kernel, out_shape=(jax.ShapeDtypeStruct(eigvals.shape, bf1...  80.3 us
    div x1, other arithmetic, local_plan(): return (grad.astype(f32) / (eigvals + damping), scores.reshape(kept))  3.63 us

profile of v3, /device:TPU:0, one launch (start us, length us, event | category | flops | bytes accessed | tf_op | source)
XLA Modules:
  0.0 85.2 jit_solution(5612754134457378780)
XLA Ops:
  0.6 80.3 %shard_map.86 = (bf16[512,1024]{1,0:T(8,128)(2,1)}, f32[1,192]{1,0:T(1,128)}) custom-call(bf16[48,1024]{1,0:T(8,128)(2,1)} %q_out_hbm.1, bf16[48,4096]{1,0:T(8,128)(2,1)} %q_in_hbm.1, bf16[1024,512]{1,0:T(8,128)(2,1)} %basis_out_hbm.1, bf16[512,1024]{1,0:T(8,128)(2,1)} %basis_in_hbm.1, f32[512,1024]{1,0:T(8,128)} %eig_hbm.1, bf16[48,1024]{1,0:T(8,128)(2,1)} %t_out_hbm.1, ...), custom_call_target="tpu_custom_call" | custom-call | flops 4000000000 | bytes 10000000 | tf_op jit(solution)/shard_map/pallas_call | solution.py:305
  81.0 0.0 copy-start
  81.0 3.6 %add_divide_fusion = f32[512,1024]{1,0:T(8,128)} fusion(f32[512,1024]{1,0:T(8,128)} %eig_hbm.1, bf16[512,1024]{1,0:T(8,128)(2,1)} %get-tuple-element.4), kind=kLoop, calls=%fused_computation | loop fusion | flops 1572864 | bytes 5242880 | tf_op jit(solution)/shard_map/div | solution.py:353
  84.6 0.0 copy-done
  84.6 0.6 copy.10
Async XLA Ops:
  81.0 3.6 %copy-start = (f32[1,192]{1,0:T(1,128)S(1)}, f32[1,192]{1,0:T(1,128)}, u32[]{:S(2)}) copy-start(f32[1,192]{1,0:T(1,128)} %get-tuple-element.5) | copy-start | bytes 2308

commit v4 on v2

--- a/solution.py
+++ b/solution.py
@@ -99,7 +99,7 @@
         load.start()
 
     barrier = pltpu.get_barrier_semaphore()
-    peers = [(d, r, j) for j in cols] + [(d, j, c) for j in rows] + [other]
+    peers = [(d, r, j) for j in cols] + [(d, j, c) for j in rows] + [other] + [(e, j, c) for j in rows]
     for peer in peers:
         pl.semaphore_signal(barrier, inc=1, device_id=peer, device_id_type=pl.DeviceIdType.MESH)
     pl.semaphore_wait(barrier, len(peers))
@@ -241,6 +241,7 @@
     rotate_out_part(1)
     add_sibling(1)
     forward(fin, fin_sem, 1, e)
+    add_across(1)
 
     arrive(fin, fin_sem, 0, d)
     got(rot.at[0, away], out_sem.at[0, 2])
@@ -251,7 +252,6 @@
     grad[...] = value.astype(bf16)
     shared[...] = (value / (eig[...] + damping)).astype(bf16)
 
-    add_across(1)
     got(rot.at[1, away], out_sem.at[1, 2])
     mixed = dot(flat(rot[1]), shared[...])
     arrive(fin, fin_sem, 1, d)
@@ -269,15 +269,18 @@
         send(part, col_sc.at[c], sc_sem.at[c], (d, r, j))
     for j in cols:
         got(col_sc.at[j], sc_sem.at[j])
-    row_sc[r] = ((col_sc[0] + col_sc[1]) + col_sc[2]) + col_sc[3]
-    for j in rows:
-        send(row_sc.at[r], row_sc.at[r], sc_sem.at[4 + r], (d, j, c))
-    for j in rows:
-        got(row_sc.at[j], sc_sem.at[4 + j])
-    dp_sc[0:2] = ((row_sc[0] + row_sc[1]) + row_sc[2]) + row_sc[3]
-    send(dp_sc.at[e], dp_sc.at[2], sc_sem.at[8], other)
-    got(dp_sc.at[2], sc_sem.at[8])
-    scores[...] = dp_sc[d, 0:1] + dp_sc[2, 0:1]
+    dp_sc[...] = ((col_sc[0] + col_sc[1]) + col_sc[2]) + col_sc[3]
+    row_sc[own_out] = dp_sc[d]
+    for half in (e, d):
+        for j in rows + [r] if half is e else rows:
+            send(dp_sc.at[half], row_sc.at[own_out], sc_sem.at[4 + own_out], (half, j, c))
+    for half in (e, d):
+        for j in rows + [r] if half is e else rows:
+            got(row_sc.at[4 * half + j], sc_sem.at[4 + 4 * half + j])
+    total = row_sc[0]
+    for at in range(1, 8):
+        total = total + row_sc[at]
+    scores[...] = total[0:1]
 
     for copy in sends:
         copy.wait_send()
@@ -323,8 +326,8 @@
             pltpu.VMEM((2, slots, own, narrow), bf16),
             pltpu.VMEM((2, 8, kept), f32),
             pltpu.VMEM((4, 2, 8, kept), f32),
-            pltpu.VMEM((4, 2, 8, kept), f32),
-            pltpu.VMEM((3, 8, kept), f32),
+            pltpu.VMEM((slots, 8, kept), f32),
+            pltpu.VMEM((2, 8, kept), f32),
             dma((11,)),
             dma((80,)),
             dma((2, 8)),
@@ -333,7 +336,7 @@
             dma((2, 8)),
             dma((2, 8)),
             dma((2, 3)),
-            dma((9,)),
+            dma((12,)),
         ],
         compiler_params=pltpu.CompilerParams(
             collective_id=0, has_side_effects=True, vmem_limit_bytes=63 * 2**20

time: 82.5 us -> 81.2 us (0.984)
  Pallas kernels: 77.5 us -> 76.2 us
    pallas_call x1, Pallas kernels: 77.5 us -> 76.2 us  [local_plan(): pl.pallas_call(kernel, out_shape=(jax.ShapeDtypeStruct(eigvals.shape, bf1...]
where the time goes in v4:
time: 81.2 us; the launch traced here: 81.1 us
  Pallas kernels  76.2 us (94%)
  other arithmetic  3.63 us (4%)
    pallas_call x1, Pallas kernels, local_plan(): pl.pallas_call(kernel, out_shape=(jax.ShapeDtypeStruct(eigvals.shape, bf1...  76.2 us
    div x1, other arithmetic, local_plan(): return (grad.astype(f32) / (eigvals + damping), scores.reshape(kept))  3.63 us

profile of v4, /device:TPU:0, one launch (start us, length us, event | category | flops | bytes accessed | tf_op | source)
XLA Modules:
  0.0 81.1 jit_solution(17894045934458910371)
XLA Ops:
  0.6 76.2 %shard_map.86 = (bf16[512,1024]{1,0:T(8,128)(2,1)}, f32[1,192]{1,0:T(1,128)}) custom-call(bf16[48,1024]{1,0:T(8,128)(2,1)} %q_out_hbm.1, bf16[48,4096]{1,0:T(8,128)(2,1)} %q_in_hbm.1, bf16[1024,512]{1,0:T(8,128)(2,1)} %basis_out_hbm.1, bf16[512,1024]{1,0:T(8,128)(2,1)} %basis_in_hbm.1, f32[512,1024]{1,0:T(8,128)} %eig_hbm.1, bf16[48,1024]{1,0:T(8,128)(2,1)} %t_out_hbm.1, ...), custom_call_target="tpu_custom_call" | custom-call | flops 4000000000 | bytes 10000000 | tf_op jit(solution)/shard_map/pallas_call | solution.py:298
  76.9 0.0 copy-start
  76.9 3.6 %add_divide_fusion = f32[512,1024]{1,0:T(8,128)} fusion(f32[512,1024]{1,0:T(8,128)} %eig_hbm.1, bf16[512,1024]{1,0:T(8,128)(2,1)} %get-tuple-element.4), kind=kLoop, calls=%fused_computation | loop fusion | flops 1572864 | bytes 5242880 | tf_op jit(solution)/shard_map/div | solution.py:346
  80.5 0.0 copy-done
  80.5 0.6 copy.10
Async XLA Ops:
  76.9 3.6 %copy-start = (f32[1,192]{1,0:T(1,128)S(1)}, f32[1,192]{1,0:T(1,128)}, u32[]{:S(2)}) copy-start(f32[1,192]{1,0:T(1,128)} %get-tuple-element.5) | copy-start | bytes 2308
